TPU v7x, 32 devices: a whole 2x2x4 slice. The times are simulated.
32 devices in a mesh: blk: 16 (over z, y, x), col: 2 (over core).
Axes of the slice: x: 2, y: 2, z: 4, core: 2. Of those that a mesh axis runs over, the one named last changes fastest.
Arguments:
- embeddings: bfloat16 [6144, 768], P('blk'), may hold values from -1 to 1
- labels: int32 [6144], P('blk'), may hold values from 0 to 999
- landmarks: bfloat16 [512, 768], P(('blk', 'col')), may hold values from -1 to 1
- coeffs: bfloat16 [512, 1000], P(('blk', 'col')), may hold values from -1.25 to 1.25
- widths: bfloat16 [512], P(('blk', 'col')), may hold values from 0.5 to 2
Outputs:
- grad_landmarks: float32 [512, 768], P(('blk', 'col'))
- grad_coeffs: float32 [512, 1000], P(('blk', 'col'))
- grad_embeddings: float32 [6144, 768], P(('blk', 'col'))
All inputs are finite; a program needn't handle non-finite values.
Results may differ from a plain program's by a relative error of at most 0.0078.
Values may be sent and summed in bfloat16 or wider, within the bound.
A program may use at most 64 MiB of HBM per device.

v0:
```python
import functools

import jax
import jax.numpy as jnp
from jax import lax
from jax.experimental import pallas as pl
from jax.experimental.pallas import tpu as pltpu
from jax.sharding import PartitionSpec as P


def from_behind(block, axis, distance):
    devices = range(lax.axis_size(axis))
    route = [((i - distance) % len(devices), i) for i in devices]
    return lax.ppermute(block, axis, route)


def block_kernel(rows, rows_sq, land, width):
    cross = lax.dot_general(
        land, rows, (((1,), (1,)), ((), ())), preferred_element_type=jnp.float32
    )
    land_sq = jnp.sum(jnp.square(land.astype(jnp.float32)), axis=1)
    dist = rows_sq[None, :] + land_sq[:, None] - 2.0 * cross
    return jnp.exp(-width.astype(jnp.float32)[:, None] * dist).astype(jnp.bfloat16)


def class_logits(kern_t, coef):
    return lax.dot_general(
        kern_t, coef, (((0,), (0,)), ((), ())), preferred_element_type=jnp.float32
    )


def logit_gradient(logits, labels):
    top = jnp.max(logits, axis=1, keepdims=True)
    expo = jnp.exp(logits - top)
    probs = expo / jnp.sum(expo, axis=1, keepdims=True)
    classes = lax.broadcasted_iota(jnp.int32, logits.shape, 1)
    onehot = (classes == labels[:, None]).astype(jnp.float32)
    return (probs - onehot).astype(jnp.bfloat16)


def grad_terms(land, coef, width, kern_t, rows, grad_rows):
    grad_kernel = lax.dot_general(
        coef, grad_rows, (((1,), (1,)), ((), ())), preferred_element_type=jnp.float32
    )
    pull = (
        2.0 * width.astype(jnp.float32)[:, None] * grad_kernel * kern_t.astype(jnp.float32)
    ).astype(jnp.bfloat16)
    grad_coef = jnp.dot(kern_t, grad_rows, preferred_element_type=jnp.float32)
    grad_land = jnp.dot(pull, rows, preferred_element_type=jnp.float32) - jnp.sum(
        pull.astype(jnp.float32), axis=1
    )[:, None] * land.astype(jnp.float32)
    return (grad_land, grad_coef, pull)


def project_rows(pull, land):
    return lax.dot_general(pull, land, (((0,), (0,)), ((), ())), preferred_element_type=jnp.float32)


def target_block(position, step, blocks):
    return (position - step - 1) % blocks


def local(embeddings, labels, landmarks, coeffs, widths):
    rows_sq = jnp.sum(jnp.square(embeddings.astype(jnp.float32)), axis=1)
    width_d = embeddings.shape[1]
    classes = coeffs.shape[1]
    size_b = landmarks.shape[0]
    blocks = lax.axis_size("blk")
    position = lax.axis_index("blk")
    all_land, all_coef, all_width = (
        lax.all_gather(landmarks, "blk", axis=0, tiled=True),
        lax.all_gather(coeffs, "blk", axis=0, tiled=True),
        lax.all_gather(widths, "blk", axis=0, tiled=True),
    )
    kern_all = block_kernel(embeddings, rows_sq, all_land, all_width)
    partial_value = class_logits(kern_all, all_coef)
    logits = lax.psum(partial_value, "col")
    grad_rows = logit_gradient(logits, labels)
    sections = ((True, 0, size_b),)

    def pass_on(values):
        return from_behind((values[0], values[1]), "blk", 1)

    empty = tuple(
        (
            (jnp.zeros((size, width_d), jnp.float32), jnp.zeros((size, classes), jnp.float32))
            for upward, low, size in sections
        )
    )
    land_all, coef_all, pull_all = grad_terms(
        all_land, all_coef, all_width, kern_all, embeddings, grad_rows
    )
    pull_z = project_rows(pull_all, all_land)
    pull_rows = jnp.sum(pull_all.astype(jnp.float32), axis=0)

    def select(values, block, low, size):
        return lax.dynamic_slice_in_dim(values, block * size_b + low, size, 0)

    def cached_step(step, accums):
        moved = []
        for index, (upward, low, size) in enumerate(sections):
            block = target_block(position, step, blocks)
            total = (
                accums[index][0] + select(land_all, block, low, size),
                accums[index][1] + select(coef_all, block, low, size),
            )
            moved.append(pass_on(total))
        return tuple(moved)

    accums = lax.fori_loop(0, blocks - 1, cached_step, empty)
    finals = [
        (
            accums[index][0] + select(land_all, position, low, size),
            accums[index][1] + select(coef_all, position, low, size),
        )
        for index, (upward, low, size) in enumerate(sections)
    ]
    grad_landmarks = jnp.concatenate([item[0] for item in finals], axis=0)
    grad_coeffs = jnp.concatenate([item[1] for item in finals], axis=0)
    local_rows = pull_z - pull_rows[:, None] * embeddings.astype(jnp.float32)
    grad_embeddings = lax.psum_scatter(local_rows, "col", scatter_dimension=0, tiled=True)
    return (grad_landmarks, grad_coeffs, grad_embeddings)


NT = (((1,), (1,)), ((), ()))
TN = (((0,), (0,)), ((), ()))


def fused_kernel(
    classes, emb_hbm, lab_hbm, land_hbm, coef_hbm, width_hbm,
    out_land, out_coef, out_emb,
    emb, lab_ref, land_ref, coef_ref, width_ref,
    table, kern, pull, pull_t, logits, grad, acc, emb_out,
    to_core, from_core, to_second, from_second, to_first, from_first, to_z, from_z,
    send_sem, z_sem, first_sem, second_sem, core_sem, back_sem, piece_sem, local_sem,
):
    blk, col = lax.axis_index("blk"), lax.axis_index("col")
    size, depth = land_ref.shape
    wide = table.shape[1]
    rows = emb.shape[0]
    slab, half = 4 * size, 8 * size
    other = 1 - col
    x, y, z = blk % 2, (blk // 2) % 2, blk // 4
    my1 = x * other + y * col
    my2 = y * other + x * col
    first = (blk + (1 - 2 * my1) * (1 + col), col)
    second = (blk + (1 - 2 * my2) * (2 - col), col)
    core = (blk, other)
    along_z = [(((z + k) % 4) * 4 + blk % 4, col) for k in range(4)]

    def base(c, p2, p1):
        return ((c * 2 + p2) * 2 + p1) * slab

    def piece(start, k):
        return pl.ds(pl.multiple_of(start + ((z - k + 4) % 4) * size, size), size)

    mine = emb_hbm.at[pl.ds(pl.multiple_of(col * rows, 64), rows)]
    loads = [
        pltpu.make_async_copy(src, dst, local_sem.at[n])
        for n, (src, dst) in enumerate((
            (land_hbm, land_ref), (coef_hbm, coef_ref), (width_hbm, width_ref),
            (lab_hbm, lab_ref), (mine, emb),
        ))
    ]
    for load in loads:
        load.start()

    barrier = pltpu.get_barrier_semaphore()
    peers = [first, second, core] + along_z[1:]
    for peer in peers:
        pl.semaphore_signal(barrier, inc=1, device_id=peer, device_id_type=pl.DeviceIdType.MESH)

    own = piece(base(col, my2, my1), 0)
    for load in loads[:3]:
        load.wait()
    eye = lax.broadcasted_iota(jnp.int32, (size, size), 0) == lax.broadcasted_iota(
        jnp.int32, (size, size), 1
    )
    width_col = jnp.sum(
        jnp.where(eye, width_ref[...].astype(jnp.float32), 0.0), axis=1, keepdims=True
    )
    tail = wide - 128
    split = tail - depth
    lanes = lax.broadcasted_iota(jnp.int32, (size, 128), 1)
    last = jnp.concatenate(
        [
            coef_ref[:, split:].astype(jnp.float32),
            jnp.zeros((size, 128 - (classes - split)), jnp.float32),
        ],
        axis=1,
    )
    last = jnp.where(lanes == classes - split, width_col, last)
    table[own, :depth] = land_ref[...]
    table[own, depth:tail] = coef_ref[:, :split]
    table[own, tail:] = last.astype(jnp.bfloat16)

    pl.semaphore_wait(barrier, len(peers))

    sends = []

    def send(src, dst, recv, device):
        copy = pltpu.make_async_remote_copy(
            src_ref=src, dst_ref=dst, send_sem=send_sem.at[len(sends)], recv_sem=recv,
            device_id=device, device_id_type=pl.DeviceIdType.MESH,
        )
        copy.start()
        sends.append(copy)

    def arrived(dst, recv):
        pltpu.make_async_remote_copy(
            src_ref=dst, dst_ref=dst, send_sem=send_sem.at[0], recv_sem=recv,
            device_id=core, device_id_type=pl.DeviceIdType.MESH,
        ).wait_recv()

    def put(where, recv, device):
        send(table.at[where], table.at[where], recv, device)

    slab_a = base(col, my2, my1)
    slab_b = base(col, my2, 1 - my1)
    slab_c = base(col, 1 - my2, my1)
    slab_d = base(col, 1 - my2, 1 - my1)
    for k in (1, 3, 2):
        put(own, z_sem.at[k], along_z[k])
    put(own, first_sem.at[0], first)
    put(own, second_sem.at[0], second)
    put(own, core_sem.at[0], core)

    for load in loads[3:]:
        load.wait()
    emb_f = emb[...].astype(jnp.float32)
    eye_rows = lax.broadcasted_iota(jnp.int32, (rows, rows), 0) == lax.broadcasted_iota(
        jnp.int32, (rows, rows), 1
    )
    rows_sq = jnp.sum(jnp.square(emb_f), axis=1, keepdims=True)
    rows_sq = jnp.sum(jnp.where(eye_rows, rows_sq, 0.0), axis=0, keepdims=True)

    for k in (1, 3, 2):
        where = piece(slab_a, k)
        arrived(table.at[where], z_sem.at[k])
        put(where, first_sem.at[k], first)
        put(where, second_sem.at[k], second)
        put(where, core_sem.at[k], core)

    def widths_of(where):
        end = table[where, tail:].astype(jnp.float32)
        at = lax.broadcasted_iota(jnp.int32, end.shape, 1) == classes - split
        return jnp.sum(jnp.where(at, end, 0.0), axis=1, keepdims=True)

    def forward(start, fresh):
        where = pl.ds(pl.multiple_of(start, half), half)
        land = table[where, :depth]
        cross = lax.dot_general(land, emb[...], NT, preferred_element_type=jnp.float32)
        land_sq = jnp.sum(jnp.square(land.astype(jnp.float32)), axis=1, keepdims=True)
        dist = (rows_sq + land_sq) - 2.0 * cross
        value = jnp.exp(-widths_of(where) * dist).astype(jnp.bfloat16)
        kern[where, :] = value
        part = lax.dot_general(
            value, table[where, depth:], TN, preferred_element_type=jnp.float32
        )
        if fresh:
            logits[...] = part
        else:
            logits[...] += part

    for k in (0, 1, 3, 2):
        where = piece(slab_b, k)
        arrived(table.at[where], first_sem.at[k])
        put(where, second_sem.at[4 + k], second)
        put(where, core_sem.at[4 + k], core)
    forward(base(col, my2, 0), True)
    for n, start in enumerate((base(other, my1, my2), base(other, my1, 1 - my2))):
        for k in range(4):
            arrived(table.at[piece(start, k)], core_sem.at[4 * n + k])
    forward(base(other, my1, 0), False)
    for n, start in enumerate((slab_c, slab_d)):
        for k in (0, 1, 3, 2):
            where = piece(start, k)
            arrived(table.at[where], second_sem.at[4 * n + k])
            put(where, core_sem.at[8 + 4 * n + k], core)
    forward(base(col, 1 - my2, 0), False)
    for n, start in enumerate((base(other, 1 - my1, my2), base(other, 1 - my1, 1 - my2))):
        for k in range(4):
            arrived(table.at[piece(start, k)], core_sem.at[8 + 4 * n + k])
    forward(base(other, 1 - my1, 0), False)

    all_rows = lab_ref.shape[0]
    mine = lax.broadcasted_iota(jnp.int32, (rows, all_rows), 1) == (
        lax.broadcasted_iota(jnp.int32, (rows, all_rows), 0) + col * rows
    )
    label = jnp.sum(
        jnp.where(mine, lab_ref[...].astype(jnp.float32)[None, :], 0.0), axis=1, keepdims=True
    ).astype(jnp.int32)
    place = lax.broadcasted_iota(jnp.int32, logits.shape, 1)
    value = jnp.where(place < classes, logits[...], -jnp.inf)
    expo = jnp.exp(value - jnp.max(value, axis=1, keepdims=True))
    probs = expo / jnp.sum(expo, axis=1, keepdims=True)
    grad[...] = (probs - jnp.where(place == label, 1.0, 0.0)).astype(jnp.bfloat16)

    def terms(start):
        where = pl.ds(pl.multiple_of(start, half), half)
        grad_kernel = lax.dot_general(
            table[where, depth:], grad[...], NT, preferred_element_type=jnp.float32
        )
        tug = (
            2.0 * widths_of(where) * grad_kernel * kern[where, :].astype(jnp.float32)
        ).astype(jnp.bfloat16)
        pull[where, :] = tug
        land = jnp.dot(tug, emb[...], preferred_element_type=jnp.float32)
        land -= jnp.sum(tug.astype(jnp.float32), axis=1, keepdims=True) * table[
            where, :depth
        ].astype(jnp.float32)
        coef = jnp.dot(kern[where, :], grad[...], preferred_element_type=jnp.float32)
        return land, coef

    def part(index):
        return pl.ds(pl.multiple_of(index * slab, slab), slab)

    def for_core(n, p2):
        land, coef = terms(base(other, p2, 0))
        to_core[n, :, :depth] = land.astype(jnp.bfloat16)
        to_core[n, :, depth:] = coef.astype(jnp.bfloat16)
        for m, p1 in enumerate((1 - my2, my2)):
            send(
                to_core.at[n, part(p1)], from_core.at[n, part(p1)],
                back_sem.at[2 * n + m], core,
            )

    def for_self(n, p2):
        land, coef = terms(base(col, p2, 0))
        acc[n, :, :depth] = land
        acc[n, :, depth:] = coef

    def target(p1, k):
        start = p1 * slab + ((z + k) % 4) * size
        return pl.ds(pl.multiple_of(start, size), size)

    order = (2, 1, 3, 0)
    for_core(0, 1 - my1)
    for_self(0, 1 - my2)
    for m, p1 in enumerate((1 - my1, my1)):
        arrived(from_core.at[0, part(p1)], back_sem.at[m])
    for n, k in enumerate(order):
        for m, p1 in enumerate((1 - my1, my1)):
            where = target(p1, k)
            total = acc[0, where, :] + from_core[0, where, :].astype(jnp.float32)
            to_second[n, m] = total.astype(jnp.bfloat16)
            send(to_second.at[n, m], from_second.at[n, m], piece_sem.at[n, m], second)
    for_core(1, my1)
    for_self(1, my2)
    for m, p1 in enumerate((1 - my1, my1)):
        arrived(from_core.at[1, part(p1)], back_sem.at[2 + m])

    def summed(n, m, p1, k):
        where = target(p1, k)
        arrived(from_second.at[n, m], piece_sem.at[n, m])
        return (
            acc[1, where, :]
            + from_core[1, where, :].astype(jnp.float32)
            + from_second[n, m].astype(jnp.float32)
        )

    def pass_first(n):
        to_first[n] = summed(n, 0, 1 - my1, order[n]).astype(jnp.bfloat16)
        send(to_first.at[n], from_first.at[n], piece_sem.at[n, 2], first)

    def collect(n):
        total = summed(n, 1, my1, order[n])
        arrived(from_first.at[n], piece_sem.at[n, 2])
        return total + from_first[n].astype(jnp.float32)

    def pass_z(n):
        to_z[n] = collect(n).astype(jnp.bfloat16)
        send(to_z.at[n], from_z.at[n], piece_sem.at[n, 3], along_z[order[n]])

    def project(n):
        where = pl.ds(n * slab, slab)
        tug = pull_t[where, :]
        drawn = jnp.dot(tug, table[:, :depth], preferred_element_type=jnp.float32)
        emb_out[where, :] = drawn - jnp.sum(
            tug.astype(jnp.float32), axis=1, keepdims=True
        ) * emb[where, :].astype(jnp.float32)

    pull_t[...] = pull[...].T
    pass_first(0)
    project(0)
    pass_first(1)
    pass_z(0)
    project(1)
    pass_first(2)
    pass_z(1)
    project(2)
    store = pltpu.make_async_copy(emb_out, out_emb, local_sem.at[5])
    store.start()
    pass_first(3)
    pass_z(2)
    result = collect(3)
    for n in (1, 2, 0):
        arrived(from_z.at[n], piece_sem.at[n, 3])
        result += from_z[n].astype(jnp.float32)
    out_land[...] = result[:, :depth]
    out_coef[...] = result[:, depth : depth + classes]

    store.wait()
    for copy in sends:
        copy.wait_send()


def place_kernel(land, coef, emb, out_land, out_coef, out_emb, sem):
    copies = [
        pltpu.make_async_copy(src, dst, sem.at[n])
        for n, (src, dst) in enumerate(((emb, out_emb), (coef, out_coef), (land, out_land)))
    ]
    for copy in copies:
        copy.start()
    for copy in copies:
        copy.wait()


def fused(embeddings, labels, landmarks, coeffs, widths):
    size, depth = landmarks.shape
    classes = coeffs.shape[1]
    rows = embeddings.shape[0] // 2
    padded = (classes // 128 + 1) * 128
    wide = depth + padded
    count, half = 32 * size, 8 * size
    vmem = pl.BlockSpec(memory_space=pltpu.VMEM)
    hbm = pl.BlockSpec(memory_space=pltpu.HBM)
    anywhere = pl.BlockSpec(memory_space=pl.ANY)
    bf16, f32 = jnp.bfloat16, jnp.float32
    out_shape = (
        jax.ShapeDtypeStruct((size, depth), f32),
        jax.ShapeDtypeStruct((size, classes), f32),
        jax.ShapeDtypeStruct((rows, depth), f32),
    )
    results = pl.pallas_call(
        functools.partial(fused_kernel, classes),
        out_shape=out_shape,
        in_specs=[hbm] * 5,
        out_specs=(vmem, vmem, anywhere),
        scratch_shapes=[
            pltpu.VMEM((rows, depth), bf16),
            pltpu.VMEM(labels.shape, labels.dtype),
            pltpu.VMEM(landmarks.shape, bf16),
            pltpu.VMEM(coeffs.shape, bf16),
            pltpu.VMEM((1, size), bf16),
            pltpu.VMEM((count, wide), bf16),
            pltpu.VMEM((count, rows), bf16),
            pltpu.VMEM((count, rows), bf16),
            pltpu.VMEM((rows, count), bf16),
            pltpu.VMEM((rows, padded), f32),
            pltpu.VMEM((rows, padded), bf16),
            pltpu.VMEM((2, half, wide), f32),
            pltpu.VMEM((rows, depth), f32),
            pltpu.VMEM((2, half, wide), bf16),
            pltpu.VMEM((2, half, wide), bf16),
            pltpu.VMEM((4, 2, size, wide), bf16),
            pltpu.VMEM((4, 2, size, wide), bf16),
            pltpu.VMEM((4, size, wide), bf16),
            pltpu.VMEM((4, size, wide), bf16),
            pltpu.VMEM((3, size, wide), bf16),
            pltpu.VMEM((3, size, wide), bf16),
            pltpu.SemaphoreType.DMA((50,)),
            pltpu.SemaphoreType.DMA((4,)),
            pltpu.SemaphoreType.DMA((4,)),
            pltpu.SemaphoreType.DMA((8,)),
            pltpu.SemaphoreType.DMA((16,)),
            pltpu.SemaphoreType.DMA((4,)),
            pltpu.SemaphoreType.DMA((4, 4)),
            pltpu.SemaphoreType.DMA((6,)),
        ],
        compiler_params=pltpu.CompilerParams(
            collective_id=0, has_side_effects=True, vmem_limit_bytes=60 * 2**20
        ),
    )(embeddings, labels, landmarks, coeffs, widths[None, :])
    return pl.pallas_call(
        place_kernel,
        out_shape=out_shape,
        in_specs=[anywhere] * 3,
        out_specs=(anywhere,) * 3,
        scratch_shapes=[pltpu.SemaphoreType.DMA((3,))],
        compiler_params=pltpu.CompilerParams(vmem_limit_bytes=60 * 2**20),
    )(*results)


def fits_fused(mesh):
    return mesh.shape["blk"] == 16 and mesh.shape["col"] == 2


def solution(mesh):
    return jax.shard_map(
        fused if fits_fused(mesh) else local,
        mesh=mesh,
        in_specs=(
            P("blk", None),
            P("blk"),
            P(("blk", "col"), None),
            P(("blk", "col"), None),
            P(("blk", "col")),
        ),
        out_specs=(P(("blk", "col"), None), P(("blk", "col"), None), P(("blk", "col"), None)),
        check_vma=False,
    )
```

profile of v0, /device:TPU:0, one launch (start us, length us, event | category | flops | bytes accessed | tf_op | source)
XLA Modules:
  0.0 61.3 jit_solution(5868249410674919241)
XLA Ops:
  0.6 38.2 %shard_map.76 = (f32[16,768]{1,0:T(8,128)}, f32[16,1000]{1,0:T(8,128)}, f32[192,768]{1,0:T(8,128)}) custom-call(bf16[384,768]{1,0:T(8,128)(2,1)} %emb_hbm.1, s32[384]{0:T(512)} %lab_hbm.1, bf16[16,768]{1,0:T(8,128)(2,1)} %land_hbm.1, bf16[16,1000]{1,0:T(8,128)(2,1)} %coef_hbm.1, bf16[1,16]{1,0:T(2,128)(2,1)} %bitcast.1), custom_call_target="tpu_custom_call" | custom-call | tf_op jit(solution)/shard_map/pallas_call | solution.py:435
  38.8 22.5 %shard_map.77 = (f32[16,768]{1,0:T(8,128)}, f32[16,1000]{1,0:T(8,128)}, f32[192,768]{1,0:T(8,128)}) custom-call(f32[16,768]{1,0:T(8,128)} %get-tuple-element.6.land, f32[16,1000]{1,0:T(8,128)} %get-tuple-element.7.coef, f32[192,768]{1,0:T(8,128)} %get-tuple-element.8.emb), custom_call_target="tpu_custom_call" | custom-call | tf_op jit(solution)/shard_map/pallas_call | solution.py:475
where the time goes:
time: 61.4 us; the launch traced here: 61.3 us
  Pallas kernels  60.7 us (99%)
  between operations  0.64 us (1%)
    pallas_call x1, Pallas kernels, fused(): pl.pallas_call(functools.partial(fused_kernel, classes), out_shape=out_sh...  38.2 us
    pallas_call x1, Pallas kernels, fused(): pl.pallas_call(place_kernel, out_shape=out_shape, in_specs=[anywhere] * 3...  22.5 us

commit v1 on v0

--- a/solution.py
+++ b/solution.py
@@ -132,7 +132,7 @@
     emb, lab_ref, land_ref, coef_ref, width_ref,
     table, kern, pull, pull_t, logits, grad, acc, emb_out,
     to_core, from_core, to_second, from_second, to_first, from_first, to_z, from_z,
-    send_sem, z_sem, first_sem, second_sem, core_sem, back_sem, piece_sem, local_sem,
+    send_sem, z_sem, first_sem, second_sem, core_sem, back_sem, piece_sem, back_z_sem, local_sem,
 ):
     blk, col = lax.axis_index("blk"), lax.axis_index("col")
     size, depth = land_ref.shape
@@ -146,13 +146,19 @@
     first = (blk + (1 - 2 * my1) * (1 + col), col)
     second = (blk + (1 - 2 * my2) * (2 - col), col)
     core = (blk, other)
-    along_z = [(((z + k) % 4) * 4 + blk % 4, col) for k in range(4)]
+    far = z // 2
+    toward = 1 - 2 * far
+    within = z + far * (3 - 2 * z)
+    nearest = [3 * far + toward * at for at in (1 - within, 2, 3)]
+
+    def at_z(where):
+        return where * 4 + blk % 4, col
 
     def base(c, p2, p1):
         return ((c * 2 + p2) * 2 + p1) * slab
 
-    def piece(start, k):
-        return pl.ds(pl.multiple_of(start + ((z - k + 4) % 4) * size, size), size)
+    def piece(start, where):
+        return pl.ds(pl.multiple_of(start + where * size, size), size)
 
     mine = emb_hbm.at[pl.ds(pl.multiple_of(col * rows, 64), rows)]
     loads = [
@@ -166,11 +172,11 @@
         load.start()
 
     barrier = pltpu.get_barrier_semaphore()
-    peers = [first, second, core] + along_z[1:]
+    peers = [first, second, core] + [at_z(where) for where in nearest]
     for peer in peers:
         pl.semaphore_signal(barrier, inc=1, device_id=peer, device_id_type=pl.DeviceIdType.MESH)
 
-    own = piece(base(col, my2, my1), 0)
+    own = piece(base(col, my2, my1), z)
     for load in loads[:3]:
         load.wait()
     eye = lax.broadcasted_iota(jnp.int32, (size, size), 0) == lax.broadcasted_iota(
@@ -219,10 +225,10 @@
     slab_b = base(col, my2, 1 - my1)
     slab_c = base(col, 1 - my2, my1)
     slab_d = base(col, 1 - my2, 1 - my1)
-    for k in (1, 3, 2):
-        put(own, z_sem.at[k], along_z[k])
+    for where in nearest:
+        put(own, z_sem.at[z], at_z(where))
+    put(own, second_sem.at[0], second)
     put(own, first_sem.at[0], first)
-    put(own, second_sem.at[0], second)
     put(own, core_sem.at[0], core)
 
     for load in loads[3:]:
@@ -234,9 +240,10 @@
     rows_sq = jnp.sum(jnp.square(emb_f), axis=1, keepdims=True)
     rows_sq = jnp.sum(jnp.where(eye_rows, rows_sq, 0.0), axis=0, keepdims=True)
 
-    for k in (1, 3, 2):
-        where = piece(slab_a, k)
-        arrived(table.at[where], z_sem.at[k])
+    around = [z] + nearest
+    for k in (1, 2, 3):
+        where = piece(slab_a, around[k])
+        arrived(table.at[where], z_sem.at[around[k]])
         put(where, first_sem.at[k], first)
         put(where, second_sem.at[k], second)
         put(where, core_sem.at[k], core)
@@ -262,25 +269,25 @@
         else:
             logits[...] += part
 
-    for k in (0, 1, 3, 2):
-        where = piece(slab_b, k)
+    for k in range(4):
+        where = piece(slab_b, around[k])
         arrived(table.at[where], first_sem.at[k])
         put(where, second_sem.at[4 + k], second)
         put(where, core_sem.at[4 + k], core)
     forward(base(col, my2, 0), True)
     for n, start in enumerate((base(other, my1, my2), base(other, my1, 1 - my2))):
         for k in range(4):
-            arrived(table.at[piece(start, k)], core_sem.at[4 * n + k])
+            arrived(table.at[piece(start, around[k])], core_sem.at[4 * n + k])
     forward(base(other, my1, 0), False)
     for n, start in enumerate((slab_c, slab_d)):
-        for k in (0, 1, 3, 2):
-            where = piece(start, k)
+        for k in range(4):
+            where = piece(start, around[k])
             arrived(table.at[where], second_sem.at[4 * n + k])
             put(where, core_sem.at[8 + 4 * n + k], core)
     forward(base(col, 1 - my2, 0), False)
     for n, start in enumerate((base(other, 1 - my1, my2), base(other, 1 - my1, 1 - my2))):
         for k in range(4):
-            arrived(table.at[piece(start, k)], core_sem.at[8 + 4 * n + k])
+            arrived(table.at[piece(start, around[k])], core_sem.at[8 + 4 * n + k])
     forward(base(other, 1 - my1, 0), False)
 
     all_rows = lab_ref.shape[0]
@@ -330,11 +337,11 @@
         acc[n, :, :depth] = land
         acc[n, :, depth:] = coef
 
-    def target(p1, k):
-        start = p1 * slab + ((z + k) % 4) * size
+    def target(p1, where):
+        start = p1 * slab + where * size
         return pl.ds(pl.multiple_of(start, size), size)
 
-    order = (2, 1, 3, 0)
+    order = around[::-1]
     for_core(0, 1 - my1)
     for_self(0, 1 - my2)
     for m, p1 in enumerate((1 - my1, my1)):
@@ -370,7 +377,7 @@
 
     def pass_z(n):
         to_z[n] = collect(n).astype(jnp.bfloat16)
-        send(to_z.at[n], from_z.at[n], piece_sem.at[n, 3], along_z[order[n]])
+        send(to_z.at[n], from_z.at[z], back_z_sem.at[z], at_z(order[n]))
 
     def project(n):
         where = pl.ds(n * slab, slab)
@@ -394,9 +401,9 @@
     pass_first(3)
     pass_z(2)
     result = collect(3)
-    for n in (1, 2, 0):
-        arrived(from_z.at[n], piece_sem.at[n, 3])
-        result += from_z[n].astype(jnp.float32)
+    for where in order[:3]:
+        arrived(from_z.at[where], back_z_sem.at[where])
+        result += from_z[where].astype(jnp.float32)
     out_land[...] = result[:, :depth]
     out_coef[...] = result[:, depth : depth + classes]
 
@@ -405,15 +412,23 @@
         copy.wait_send()
 
 
-def place_kernel(land, coef, emb, out_land, out_coef, out_emb, sem):
-    copies = [
-        pltpu.make_async_copy(src, dst, sem.at[n])
-        for n, (src, dst) in enumerate(((emb, out_emb), (coef, out_coef), (land, out_land)))
+def place_kernel(emb, coef, land, out_emb, out_coef, out_land, held_emb, held_coef, held_land, sem):
+    held = (held_emb, held_coef, held_land)
+    loads = [
+        pltpu.make_async_copy(src, dst, sem.at[0, n])
+        for n, (src, dst) in enumerate(zip((emb, coef, land), held))
     ]
-    for copy in copies:
-        copy.start()
-    for copy in copies:
-        copy.wait()
+    stores = [
+        pltpu.make_async_copy(src, dst, sem.at[1, n])
+        for n, (src, dst) in enumerate(zip(held, (out_emb, out_coef, out_land)))
+    ]
+    for load in loads:
+        load.start()
+    for load, store in zip(loads, stores):
+        load.wait()
+        store.start()
+    for store in stores:
+        store.wait()
 
 
 def fused(embeddings, labels, landmarks, coeffs, widths):
@@ -458,28 +473,31 @@
             pltpu.VMEM((4, size, wide), bf16),
             pltpu.VMEM((4, size, wide), bf16),
             pltpu.VMEM((3, size, wide), bf16),
-            pltpu.VMEM((3, size, wide), bf16),
+            pltpu.VMEM((4, size, wide), bf16),
             pltpu.SemaphoreType.DMA((50,)),
             pltpu.SemaphoreType.DMA((4,)),
             pltpu.SemaphoreType.DMA((4,)),
             pltpu.SemaphoreType.DMA((8,)),
             pltpu.SemaphoreType.DMA((16,)),
             pltpu.SemaphoreType.DMA((4,)),
-            pltpu.SemaphoreType.DMA((4, 4)),
+            pltpu.SemaphoreType.DMA((4, 3)),
+            pltpu.SemaphoreType.DMA((4,)),
             pltpu.SemaphoreType.DMA((6,)),
         ],
         compiler_params=pltpu.CompilerParams(
             collective_id=0, has_side_effects=True, vmem_limit_bytes=60 * 2**20
         ),
     )(embeddings, labels, landmarks, coeffs, widths[None, :])
-    return pl.pallas_call(
+    grad_emb, grad_coef, grad_land = pl.pallas_call(
         place_kernel,
-        out_shape=out_shape,
+        out_shape=out_shape[::-1],
         in_specs=[anywhere] * 3,
         out_specs=(anywhere,) * 3,
-        scratch_shapes=[pltpu.SemaphoreType.DMA((3,))],
+        scratch_shapes=[pltpu.VMEM(out.shape, out.dtype) for out in out_shape[::-1]]
+        + [pltpu.SemaphoreType.DMA((2, 3))],
         compiler_params=pltpu.CompilerParams(vmem_limit_bytes=60 * 2**20),
-    )(*results)
+    )(*results[::-1])
+    return grad_land, grad_coef, grad_emb
 
 
 def fits_fused(mesh):

time: 61.4 us -> 40.7 us (0.66)
  Pallas kernels: 60.7 us -> 40 us
    pallas_call x1, Pallas kernels: 22.5 us -> 1.95 us  [fused(): pl.pallas_call(place_kernel, out_shape=out_shape[::-1], in_specs=[anywher...]
where the time goes in v1:
time: 40.7 us; the launch traced here: 40.6 us
  Pallas kernels  40 us (98%)
  between operations  0.64 us (2%)
    pallas_call x1, Pallas kernels, fused(): pl.pallas_call(functools.partial(fused_kernel, classes), out_shape=out_sh...  38 us
    pallas_call x1, Pallas kernels, fused(): pl.pallas_call(place_kernel, out_shape=out_shape[::-1], in_specs=[anywher...  1.95 us

profile of v1, /device:TPU:0, one launch (start us, length us, event | category | flops | bytes accessed | tf_op | source)
XLA Modules:
  0.0 40.6 jit_solution(13646326632726018927)
XLA Ops:
  0.6 38.0 %shard_map.76 = (f32[16,768]{1,0:T(8,128)}, f32[16,1000]{1,0:T(8,128)}, f32[192,768]{1,0:T(8,128)}) custom-call(bf16[384,768]{1,0:T(8,128)(2,1)} %emb_hbm.1, s32[384]{0:T(512)} %lab_hbm.1, bf16[16,768]{1,0:T(8,128)(2,1)} %land_hbm.1, bf16[16,1000]{1,0:T(8,128)(2,1)} %coef_hbm.1, bf16[1,16]{1,0:T(2,128)(2,1)} %bitcast.1), custom_call_target="tpu_custom_call" | custom-call | tf_op jit(solution)/shard_map/pallas_call | solution.py:450
  38.6 2.0 %shard_map.77 = (f32[192,768]{1,0:T(8,128)}, f32[16,1000]{1,0:T(8,128)}, f32[16,768]{1,0:T(8,128)}) custom-call(f32[192,768]{1,0:T(8,128)} %get-tuple-element.9.emb, f32[16,1000]{1,0:T(8,128)} %get-tuple-element.10.coef, f32[16,768]{1,0:T(8,128)} %get-tuple-element.11.land), custom_call_target="tpu_custom_call" | custom-call | tf_op jit(solution)/shard_map/pallas_call | solution.py:491

commit v2 on v1

--- a/solution.py
+++ b/solution.py
@@ -130,9 +130,9 @@
     classes, emb_hbm, lab_hbm, land_hbm, coef_hbm, width_hbm,
     out_land, out_coef, out_emb,
     emb, lab_ref, land_ref, coef_ref, width_ref,
-    table, kern, pull, pull_t, logits, grad, acc, emb_out,
+    table, kern, pull, pull_t, logits, grad, acc,
     to_core, from_core, to_second, from_second, to_first, from_first, to_z, from_z,
-    send_sem, z_sem, first_sem, second_sem, core_sem, back_sem, piece_sem, back_z_sem, local_sem,
+    send_sem, z_sem, first_sem, second_sem, core_sem, back_sem, piece_sem, back_z_sem, pair_sem, local_sem,
 ):
     blk, col = lax.axis_index("blk"), lax.axis_index("col")
     size, depth = land_ref.shape
@@ -245,7 +245,8 @@
         where = piece(slab_a, around[k])
         arrived(table.at[where], z_sem.at[around[k]])
         put(where, first_sem.at[k], first)
-        put(where, second_sem.at[k], second)
+        if k != 1:
+            put(where, second_sem.at[k], second)
         put(where, core_sem.at[k], core)
 
     def widths_of(where):
@@ -272,7 +273,8 @@
     for k in range(4):
         where = piece(slab_b, around[k])
         arrived(table.at[where], first_sem.at[k])
-        put(where, second_sem.at[4 + k], second)
+        if k != 1:
+            put(where, second_sem.at[4 + k], second)
         put(where, core_sem.at[4 + k], core)
     forward(base(col, my2, 0), True)
     for n, start in enumerate((base(other, my1, my2), base(other, my1, 1 - my2))):
@@ -280,9 +282,11 @@
             arrived(table.at[piece(start, around[k])], core_sem.at[4 * n + k])
     forward(base(other, my1, 0), False)
     for n, start in enumerate((slab_c, slab_d)):
-        for k in range(4):
+        for k in (0, 2, 3, 1):
             where = piece(start, around[k])
-            arrived(table.at[where], second_sem.at[4 * n + k])
+            arrived(table.at[where], pair_sem.at[n] if k == 1 else second_sem.at[4 * n + k])
+            if k == 0:
+                put(where, pair_sem.at[n], at_z(around[1]))
             put(where, core_sem.at[8 + 4 * n + k], core)
     forward(base(col, 1 - my2, 0), False)
     for n, start in enumerate((base(other, 1 - my1, my2), base(other, 1 - my1, 1 - my2))):
@@ -346,12 +350,18 @@
     for_self(0, 1 - my2)
     for m, p1 in enumerate((1 - my1, my1)):
         arrived(from_core.at[0, part(p1)], back_sem.at[m])
-    for n, k in enumerate(order):
+    for n in (2, 0, 1, 3):
         for m, p1 in enumerate((1 - my1, my1)):
-            where = target(p1, k)
+            where = target(p1, order[n])
             total = acc[0, where, :] + from_core[0, where, :].astype(jnp.float32)
+            if n == 3:
+                arrived(from_second.at[2, m], piece_sem.at[2, m])
+                total += from_second[2, m].astype(jnp.float32)
             to_second[n, m] = total.astype(jnp.bfloat16)
-            send(to_second.at[n, m], from_second.at[n, m], piece_sem.at[n, m], second)
+            send(
+                to_second.at[n, m], from_second.at[n, m], piece_sem.at[n, m],
+                at_z(order[2]) if n == 2 else second,
+            )
     for_core(1, my1)
     for_self(1, my2)
     for m, p1 in enumerate((1 - my1, my1)):
@@ -359,12 +369,11 @@
 
     def summed(n, m, p1, k):
         where = target(p1, k)
-        arrived(from_second.at[n, m], piece_sem.at[n, m])
-        return (
-            acc[1, where, :]
-            + from_core[1, where, :].astype(jnp.float32)
-            + from_second[n, m].astype(jnp.float32)
-        )
+        total = acc[1, where, :] + from_core[1, where, :].astype(jnp.float32)
+        if n != 2:
+            arrived(from_second.at[n, m], piece_sem.at[n, m])
+            total += from_second[n, m].astype(jnp.float32)
+        return total
 
     def pass_first(n):
         to_first[n] = summed(n, 0, 1 - my1, order[n]).astype(jnp.bfloat16)
@@ -383,7 +392,7 @@
         where = pl.ds(n * slab, slab)
         tug = pull_t[where, :]
         drawn = jnp.dot(tug, table[:, :depth], preferred_element_type=jnp.float32)
-        emb_out[where, :] = drawn - jnp.sum(
+        out_emb[where, :] = drawn - jnp.sum(
             tug.astype(jnp.float32), axis=1, keepdims=True
         ) * emb[where, :].astype(jnp.float32)
 
@@ -396,8 +405,6 @@
     pass_first(2)
     pass_z(1)
     project(2)
-    store = pltpu.make_async_copy(emb_out, out_emb, local_sem.at[5])
-    store.start()
     pass_first(3)
     pass_z(2)
     result = collect(3)
@@ -407,25 +414,16 @@
     out_land[...] = result[:, :depth]
     out_coef[...] = result[:, depth : depth + classes]
 
-    store.wait()
     for copy in sends:
         copy.wait_send()
 
 
-def place_kernel(emb, coef, land, out_emb, out_coef, out_land, held_emb, held_coef, held_land, sem):
-    held = (held_emb, held_coef, held_land)
-    loads = [
-        pltpu.make_async_copy(src, dst, sem.at[0, n])
-        for n, (src, dst) in enumerate(zip((emb, coef, land), held))
+def place_kernel(emb, coef, land, out_emb, out_coef, out_land, sem):
+    stores = [
+        pltpu.make_async_copy(src, dst, sem.at[n])
+        for n, (src, dst) in enumerate(((emb, out_emb), (coef, out_coef), (land, out_land)))
     ]
-    stores = [
-        pltpu.make_async_copy(src, dst, sem.at[1, n])
-        for n, (src, dst) in enumerate(zip(held, (out_emb, out_coef, out_land)))
-    ]
-    for load in loads:
-        load.start()
-    for load, store in zip(loads, stores):
-        load.wait()
+    for store in stores:
         store.start()
     for store in stores:
         store.wait()
@@ -449,9 +447,9 @@
     )
     results = pl.pallas_call(
         functools.partial(fused_kernel, classes),
-        out_shape=out_shape,
+        out_shape=tuple(pltpu.VMEM(out.shape, out.dtype) for out in out_shape),
         in_specs=[hbm] * 5,
-        out_specs=(vmem, vmem, anywhere),
+        out_specs=(vmem,) * 3,
         scratch_shapes=[
             pltpu.VMEM((rows, depth), bf16),
             pltpu.VMEM(labels.shape, labels.dtype),
@@ -465,7 +463,6 @@
             pltpu.VMEM((rows, padded), f32),
             pltpu.VMEM((rows, padded), bf16),
             pltpu.VMEM((2, half, wide), f32),
-            pltpu.VMEM((rows, depth), f32),
             pltpu.VMEM((2, half, wide), bf16),
             pltpu.VMEM((2, half, wide), bf16),
             pltpu.VMEM((4, 2, size, wide), bf16),
@@ -482,7 +479,8 @@
             pltpu.SemaphoreType.DMA((4,)),
             pltpu.SemaphoreType.DMA((4, 3)),
             pltpu.SemaphoreType.DMA((4,)),
-            pltpu.SemaphoreType.DMA((6,)),
+            pltpu.SemaphoreType.DMA((2,)),
+            pltpu.SemaphoreType.DMA((5,)),
         ],
         compiler_params=pltpu.CompilerParams(
             collective_id=0, has_side_effects=True, vmem_limit_bytes=60 * 2**20
@@ -491,11 +489,10 @@
     grad_emb, grad_coef, grad_land = pl.pallas_call(
         place_kernel,
         out_shape=out_shape[::-1],
-        in_specs=[anywhere] * 3,
+        in_specs=[vmem] * 3,
         out_specs=(anywhere,) * 3,
-        scratch_shapes=[pltpu.VMEM(out.shape, out.dtype) for out in out_shape[::-1]]
-        + [pltpu.SemaphoreType.DMA((2, 3))],
-        compiler_params=pltpu.CompilerParams(vmem_limit_bytes=60 * 2**20),
+        scratch_shapes=[pltpu.SemaphoreType.DMA((3,))],
+        compiler_params=pltpu.CompilerParams(vmem_limit_bytes=16 * 2**20),
     )(*results[::-1])
     return grad_land, grad_coef, grad_emb
 

time: 40.7 us -> 46.1 us (1.13)
  Pallas kernels: 40 us -> 45.3 us
    pallas_call x2, Pallas kernels: 40 us -> 45.3 us  [the longest x1 44.4 us: fused(): pl.pallas_call(functools.partial(fused_kernel, classes), out_shape=tuple(...]
where the time goes in v2:
time: 46.1 us; the launch traced here: 45.9 us
  Pallas kernels  45.3 us (98%)
  between operations  0.64 us (1%)
    pallas_call x1, Pallas kernels, fused(): pl.pallas_call(functools.partial(fused_kernel, classes), out_shape=tuple(...  44.4 us

profile of v2, /device:TPU:0, one launch (start us, length us, event | category | flops | bytes accessed | tf_op | source)
XLA Modules:
  0.0 45.9 jit_solution(7279223755929675648)
XLA Ops:
  0.6 44.4 %shard_map.76 = (f32[16,768]{1,0:T(8,128)S(1)}, f32[16,1000]{1,0:T(8,128)S(1)}, f32[192,768]{1,0:T(8,128)S(1)}) custom-call(bf16[384,768]{1,0:T(8,128)(2,1)} %emb_hbm.1, s32[384]{0:T(512)} %lab_hbm.1, bf16[16,768]{1,0:T(8,128)(2,1)} %land_hbm.1, bf16[16,1000]{1,0:T(8,128)(2,1)} %coef_hbm.1, bf16[1,16]{1,0:T(2,128)(2,1)} %bitcast.1), custom_call_target="tpu_custom_call" | custom-call | tf_op jit(solution)/shard_map/pallas_call | solution.py:448
  45.1 0.9 %shard_map.77 = (f32[192,768]{1,0:T(8,128)}, f32[16,1000]{1,0:T(8,128)}, f32[16,768]{1,0:T(8,128)}) custom-call(f32[192,768]{1,0:T(8,128)S(1)} %get-tuple-element.9.emb, f32[16,1000]{1,0:T(8,128)S(1)} %get-tuple-element.10.coef, f32[16,768]{1,0:T(8,128)S(1)} %get-tuple-element.11.land), custom_call_target="tpu_custom_call" | custom-call | tf_op jit(solution)/shard_map/pallas_call | solution.py:489
